TPU v7x, 512 devices: a whole 4x8x8 slice. The times are simulated.
512 devices in a mesh: leaf: 4 (over x), row: 16 (over z, core), col: 8 (over y).
Axes of the slice: x: 4, y: 8, z: 8, core: 2. Of those that a mesh axis runs over, the one named last changes fastest.
Arguments:
- widths: int32 [15], replicated, may hold values from 1024 to 2048, as said below
- bottom_lists: int32 [8, 32], P('leaf'), may hold values from 0 to 47, as said below
- root_inverse: bfloat16 [2048, 2048], P('row')
- second_panels: bfloat16 [4, 2048, 1024], P('leaf', 'row', 'col'), may hold values from -0.09375 to 0.09375
- second_inverse: bfloat16 [4, 1024, 2048], P('leaf', 'col', 'row')
- third_panels: bfloat16 [4, 2, 2048, 2048], P('leaf', None, 'row', 'col'), may hold values from -0.09375 to 0.09375
- third_inverse: bfloat16 [4, 2048, 2048], P('leaf', 'col', 'row')
- bottom_panels: bfloat16 [8, 4096, 2048], P('leaf', 'row', 'col'), may hold values from -0.09375 to 0.09375
- bottom_inverse: bfloat16 [8, 2048, 2048], P('leaf', 'col', 'row')
Outputs:
- second_off: bfloat16 [4, 2048, 1024], P('leaf', 'row', 'col')
- second_diag: bfloat16 [4, 1024, 2048], P('leaf', 'col', 'row')
- third_off: bfloat16 [4, 2, 2048, 2048], P('leaf', None, 'row', 'col')
- third_diag: bfloat16 [4, 2048, 2048], P('leaf', 'col', 'row')
- bottom_off: bfloat16 [8, 3, 2048, 2048], P('leaf', None, 'row', 'col')
- bottom_diag: bfloat16 [8, 2048, 2048], P('leaf', 'col', 'row')
Inputs may be any that keep to these rules, and one draw needn't show every extreme that they name: `widths`: some supernode has 2048 columns and some 2048/2. `bottom_lists`: row e lists 32 different blocks of 128 rows of its chain (root, then second-level ancestor, then parent, 16 blocks each) in increasing order; block 0 and all blocks of the parent are always listed.
All inputs are finite; a program needn't handle non-finite values.
Results may differ from a plain program's by a relative error of at most 0.015.
Values may be sent and summed in bfloat16 or wider, within the bound.
A program may use at most 64 MiB of HBM per device.

v0:
```python
import jax
import jax.numpy as jnp
from jax import lax
from jax.sharding import PartitionSpec as P

NODES = 15
BOTTOM = 8


def partner(block, axis, apart):
    count = lax.axis_size(axis)
    route = []
    for low in range(count):
        high = low | 1 << apart
        if high != low and high < count:
            route += [(low, high), (high, low)]
    return lax.ppermute(block, axis, route)


def node_width(widths, node_at):
    return jnp.sum(jnp.where(jnp.arange(widths.shape[0]) == node_at, widths, 0))


def chain_fold(flat_chain, tile_width, ancestors, shard_piece):
    piece_rows = shard_piece.shape[1]
    picked = jnp.concatenate(
        [
            lax.dynamic_slice_in_dim(flat_chain, level_at * tile_width, piece_rows, 1)
            for level_at in range(ancestors)
        ],
        axis=1,
    )
    stacked = shard_piece.reshape(ancestors * piece_rows, shard_piece.shape[2])
    return jnp.dot(picked, stacked, preferred_element_type=jnp.float32)


def local(
    widths,
    bottom_lists,
    root_inverse,
    second_panels,
    second_inverse,
    third_panels,
    third_inverse,
    bottom_panels,
    bottom_inverse,
):
    group_at = lax.axis_index("leaf")
    row_at = lax.axis_index("row")
    col_at = lax.axis_index("col")
    rows_dev = root_inverse.shape[0]
    tile_width = root_inverse.shape[1]
    half_cols = second_panels.shape[2]
    own_cols = third_panels.shape[3]
    half_at = group_at % 2
    parent_one = 1 + group_at // 2
    node_two = 3 + group_at
    row_first = row_at * rows_dev
    row_index = row_first + jnp.arange(rows_dev)
    root_width = node_width(widths, 0)
    root_mask = (row_index < root_width)[:, None] & (jnp.arange(tile_width) < root_width)[None, :]
    root_block = jnp.where(root_mask, root_inverse, 0)
    width_one = node_width(widths, parent_one)
    mask_rows_one = row_index < width_one
    first_col = half_at * (tile_width // 2) + col_at * half_cols
    mask_cols_one = first_col + jnp.arange(half_cols) < width_one
    panel_one = jnp.where(mask_cols_one[None, :], second_panels[0], 0)
    flat_piece = lax.all_gather(panel_one, "row", axis=0, tiled=True)
    product_one = jnp.dot(root_block, flat_piece, preferred_element_type=jnp.float32)
    off_one = (-product_one).astype(jnp.bfloat16)
    mine_half = lax.all_gather(off_one, "col", axis=1, tiled=True)
    other_half = partner(mine_half, "leaf", 0)
    off_full = jnp.where(
        half_at == 0,
        jnp.concatenate([mine_half, other_half], 1),
        jnp.concatenate([other_half, mine_half], 1),
    )
    term_one = lax.dot_general(
        panel_one, off_full, (((0,), (0,)), ((), ())), preferred_element_type=jnp.float32
    )
    summed_one = lax.psum_scatter(
        term_one.astype(jnp.bfloat16), "row", scatter_dimension=1, tiled=True
    ).astype(jnp.float32)
    inverse_one = jnp.where(
        mask_cols_one[:, None] & mask_rows_one[None, :], second_inverse[0], 0
    ).astype(jnp.float32)
    diag_one = (inverse_one - summed_one).astype(jnp.bfloat16)
    mine_diag = lax.all_gather(diag_one.T, "col", axis=1, tiled=True)
    other_diag = partner(mine_diag, "leaf", 0)
    diag_full = jnp.where(
        half_at == 0,
        jnp.concatenate([mine_diag, other_diag], 1),
        jnp.concatenate([other_diag, mine_diag], 1),
    )
    second_off = off_one[None]
    second_diag = diag_one[None]
    turned_one = lax.all_to_all(off_full, "row", split_axis=1, concat_axis=0, tiled=True)
    chain_two = jnp.stack(
        [jnp.concatenate([root_block, off_full], 1), jnp.concatenate([turned_one.T, diag_full], 1)],
        0,
    )
    flat_two = chain_two.reshape(2 * rows_dev, 2 * tile_width)
    first_own = col_at * own_cols
    width_two = node_width(widths, node_two)
    mask_cols_two = first_own + jnp.arange(own_cols) < width_two
    panel_two = jnp.where(mask_cols_two[None, None, :], third_panels[0], 0)
    product_two = chain_fold(
        flat_two, tile_width, 2, lax.all_gather(panel_two, "row", axis=1, tiled=True)
    )
    off_two = (-product_two).astype(jnp.bfloat16).reshape(2, rows_dev, own_cols)
    full_two = lax.all_gather(off_two, "col", axis=2, tiled=True)
    term_two = jnp.einsum("kin,kim->nm", panel_two, full_two, preferred_element_type=jnp.float32)
    summed_two = lax.psum_scatter(
        term_two.astype(jnp.bfloat16), "row", scatter_dimension=1, tiled=True
    ).astype(jnp.float32)
    mask_rows_two = row_index < width_two
    inverse_two = jnp.where(
        mask_cols_two[:, None] & mask_rows_two[None, :], third_inverse[0], 0
    ).astype(jnp.float32)
    diag_two = (inverse_two - summed_two).astype(jnp.bfloat16)
    diag_rows_two = lax.all_gather(diag_two.T, "col", axis=1, tiled=True)
    turned_two = lax.all_to_all(full_two, "row", split_axis=2, concat_axis=1, tiled=True)
    lower_two = jnp.transpose(turned_two, (2, 0, 1)).reshape(rows_dev, 2 * tile_width)
    chain_three = jnp.stack(
        [
            jnp.concatenate([chain_two[0], full_two[0]], 1),
            jnp.concatenate([chain_two[1], full_two[1]], 1),
            jnp.concatenate([lower_two, diag_rows_two], 1),
        ],
        0,
    )
    flat_three = chain_three.reshape(3 * rows_dev, 3 * tile_width)
    bottom_dev = bottom_panels.shape[0]
    list_len = bottom_lists.shape[1]
    block_rows = 2 * tile_width // list_len
    node_three = NODES - BOTTOM + bottom_dev * group_at + jnp.arange(bottom_dev)
    width_three = jnp.sum(
        jnp.where(jnp.arange(widths.shape[0])[None, :] == node_three[:, None], widths[None, :], 0),
        1,
    )
    mask_cols_three = (first_own + jnp.arange(own_cols))[None, :] < width_three[:, None]
    panel_three = jnp.where(mask_cols_three[:, None, :], bottom_panels, 0)
    positions = (
        jnp.repeat(bottom_lists, block_rows, axis=1) * block_rows
        + jnp.arange(list_len * block_rows) % block_rows
    )
    own_chain = (jnp.arange(3)[:, None] * tile_width + row_index[None, :]).reshape(-1)
    matches = bottom_lists[:, :, None] == (own_chain // block_rows)[None, None, :]
    member = jnp.any(matches, axis=1)
    lower_all = lax.all_gather(panel_three, "row", axis=1, tiled=True)
    spread = jax.vmap(
        lambda where_to, values_in: jnp.zeros((3 * tile_width, own_cols), jnp.bfloat16)
        .at[where_to]
        .set(values_in)
    )(positions, lower_all)
    product_three = jnp.einsum(
        "ab,ebn->ean", flat_three, spread, preferred_element_type=jnp.float32
    )
    chain_rows = lax.dynamic_slice_in_dim(
        spread.reshape(bottom_dev, 3, tile_width, own_cols), row_first, rows_dev, 2
    )
    off_three = jnp.where(member[:, :, None], -product_three, 0.0).astype(jnp.bfloat16)
    off_three = off_three.reshape(bottom_dev, 3, rows_dev, own_cols)
    full_three = lax.all_gather(off_three, "col", axis=3, tiled=True)
    term_three = jnp.einsum(
        "ekin,ekim->enm", chain_rows, full_three, preferred_element_type=jnp.float32
    )
    summed_three = lax.psum_scatter(
        term_three.astype(jnp.bfloat16), "row", scatter_dimension=2, tiled=True
    ).astype(jnp.float32)
    mask_rows_three = row_index[None, :] < width_three[:, None]
    inverse_three = jnp.where(
        mask_cols_three[:, :, None] & mask_rows_three[:, None, :], bottom_inverse, 0
    ).astype(jnp.float32)
    diag_three = (inverse_three - summed_three).astype(jnp.bfloat16)
    return (second_off, second_diag, off_two[None], diag_two[None], off_three, diag_three)


def solution(mesh):
    in_specs = (
        P(),
        P("leaf", None),
        P("row", None),
        P("leaf", "row", "col"),
        P("leaf", "col", "row"),
        P("leaf", None, "row", "col"),
        P("leaf", "col", "row"),
        P("leaf", "row", "col"),
        P("leaf", "col", "row"),
    )
    out_specs = (
        P("leaf", "row", "col"),
        P("leaf", "col", "row"),
        P("leaf", None, "row", "col"),
        P("leaf", "col", "row"),
        P("leaf", None, "row", "col"),
        P("leaf", "col", "row"),
    )
    return jax.shard_map(local, mesh=mesh, in_specs=in_specs, out_specs=out_specs, check_vma=False)
```

profile of v0, /device:TPU:8, one launch (start us, length us, event | category | flops | bytes accessed | tf_op | source)
XLA Modules:
  0.0 519.0 jit_solution(5305973732029650270)
XLA Ops:
  8.1 1.3 fusion.20
  10.2 24.6 %all_gather.24 = bf16[2048,128]{0,1:T(8,128)(2,1)S(1)} all-gather(bf16[128,128]{0,1:T(8,128)(2,1)S(1)} %bitcast_select_fusion.1), channel_id=1, replica_groups=mesh['leaf'=4,'row'=16,'col'=8] {'row'}, dimensions={0}, use_global_device_ids=true | all-gather | bytes 557056 | tf_op jit(solution)/shard_map/all_gather | solution.py:68
  36.1 1.3 and_select_fusion
  37.7 23.5 %all_gather.25 = bf16[128,1024]{1,0:T(8,128)(2,1)S(1)} all-gather(bf16[128,128]{1,0:T(8,128)(2,1)S(1)} %fusion.7), channel_id=1, replica_groups=mesh['leaf'=4,'row'=16,'col'=8] {'col'}, dimensions={1}, use_global_device_ids=true | all-gather | bytes 294912 | tf_op jit(solution)/shard_map/all_gather | solution.py:71
  61.3 3.5 collective-permute-start
  64.8 4.9 collective-permute-done
  73.4 3.6 all-to-all-start
  77.8 49.9 %reduce-scatter.6.cloned.1.call-done = bf16[128,128]{0,1:T(8,128)(2,1)} async-done(((bf16[128,2048]{0,1:T(8,128)(2,1)}), bf16[128,128]{0,1:T(8,128)(2,1)}) %reduce-scatter.6.cloned.1.call-update) | async-done | bytes 32784 | tf_op jit(solution)/shard_map/reduce_scatter | solution.py:81
  128.6 23.1 %all_gather.26 = bf16[128,1024]{1,0:T(8,128)(2,1)S(1)} all-gather(bf16[128,128]{1,0:T(8,128)(2,1)S(1)} %get-tuple-element.37), channel_id=1, replica_groups=mesh['leaf'=4,'row'=16,'col'=8] {'col'}, dimensions={1}, use_global_device_ids=true | all-gather | bytes 294912 | tf_op jit(solution)/shard_map/all_gather | solution.py:88
  151.7 3.2 collective-permute-start.1
  155.2 4.8 collective-permute-done.1
  161.3 1.5 pad_maximum_fusion.1
  162.8 9.9 %all-gather.5.cloned.1.call-done = bf16[2,2048,256]{2,1,0:T(8,128)(2,1)} async-done(((bf16[2,128,256]{2,1,0:T(8,128)(2,1)}), bf16[2,2048,256]{2,1,0:T(8,128)(2,1)}) %all-gather.5.cloned.1.call-update) | async-done | bytes 2097168 | tf_op jit(solution)/shard_map/all_gather | solution.py:108
  172.8 3.6 fusion.6
  176.5 39.9 %all-gather.7.cloned.1.call-done = bf16[2,128,2048]{2,1,0:T(8,128)(2,1)} async-done(((bf16[2,128,256]{2,1,0:T(8,128)(2,1)}), bf16[2,128,2048]{2,1,0:T(8,128)(2,1)}) %all-gather.7.cloned.1.call-update) | async-done | bytes 1048592 | tf_op jit(solution)/shard_map/all_gather | solution.py:111
  216.4 2.8 fusion.2
  220.8 2.0 copy.69
  222.8 7.5 %all-to-all-start.1 = ((bf16[2,128,2048]{1,0,2:T(2,128)(2,1)}), bf16[2,128,2048]{1,0,2:T(2,128)(2,1)}, u32[]{:S(2)}, u32[]{:S(2)}) async-start(bf16[2,128,2048]{1,0,2:T(2,128)(2,1)} %copy.69), calls=%async_computation.3 | async-start | bytes 2097152 | tf_op jit(solution)/shard_map/all_to_all | solution.py:122
  231.5 2.3 maximum_bitcast_fusion
  233.8 24.9 %all-to-all-done.1 = bf16[2,128,2048]{1,0,2:T(2,128)(2,1)} async-done(((bf16[2,128,2048]{1,0,2:T(2,128)(2,1)}), bf16[2,128,2048]{1,0,2:T(2,128)(2,1)}, u32[]{:S(2)}, u32[]{:S(2)}) %all-to-all-start.1) | async-done | bytes 1048608 | tf_op jit(solution)/shard_map/all_to_all | solution.py:122
  258.8 1.9 copy.95
  261.1 25.3 %reduce-scatter.8.cloned.1.call-done = bf16[256,128]{0,1:T(8,128)(2,1)} async-done(((bf16[256,2048]{0,1:T(8,128)(2,1)}), bf16[256,128]{0,1:T(8,128)(2,1)}) %reduce-scatter.8.cloned.1.call-update) | async-done | bytes 65552 | tf_op jit(solution)/shard_map/reduce_scatter | solution.py:113
  287.3 25.9 %all_gather.30 = bf16[128,2048]{1,0:T(8,128)(2,1)S(1)} all-gather(bf16[128,256]{1,0:T(8,128)(2,1)S(1)} %get-tuple-element.35), channel_id=1, replica_groups=mesh['leaf'=4,'row'=16,'col'=8] {'col'}, dimensions={1}, use_global_device_ids=true | all-gather | bytes 589824 | tf_op jit(solution)/shard_map/all_gather | solution.py:121
  313.3 3.6 pad_maximum_fusion
  317.0 18.1 %all-gather.9.cloned.1.call-done = bf16[2,4096,256]{2,1,0:T(8,128)(2,1)} async-done(((bf16[2,256,256]{2,1,0:T(8,128)(2,1)}), bf16[2,4096,256]{2,1,0:T(8,128)(2,1)}) %all-gather.9.cloned.1.call-update) | async-done | bytes 4194320 | tf_op jit(solution)/shard_map/all_gather | solution.py:150
  335.1 39.1 %scatter_custom_fusion = bf16[12288,256]{1,0:T(8,128)(2,1)} fusion(s32[8192]{0:T(1024)S(1)} %bitcast.140, bf16[8192,256]{1,0:T(8,128)(2,1)} %bitcast.141, bf16[]{:T(256)} %constant.73.clone.1), kind=kCustom, calls=%fused_computation.3 | custom fusion | bytes 6291968
  374.1 7.6 %fusion.5 = bf16[2,384,256]{1,2,0:T(8,128)(2,1)S(1)} fusion(bf16[2,6144,256]{2,1,0:T(8,128)(2,1)} %bitcast.125, bf16[384,6144,1]{1,0,2:T(8,128)(2,1)} %bitcast.127, pred[2,384]{1,0:T(4,128)(4,1)S(1)} %compare_reduce_fusion), kind=kOutput, calls=%fused_computation.15 | convolution fusion | flops 2416508928 | bytes 11404032 | tf_op jit(solution)/shard_map/ab,ebn->ean/dot_general | solution.py:156
  382.7 57.5 %all-gather.11.cloned.1.call-done = bf16[2,3,128,2048]{3,2,1,0:T(8,128)(2,1)} async-done(((bf16[2,3,128,256]{3,2,1,0:T(8,128)(2,1)}), bf16[2,3,128,2048]{3,2,1,0:T(8,128)(2,1)}) %all-gather.11.cloned.1.call-update) | async-done | bytes 3145744 | tf_op jit(solution)/shard_map/all_gather | solution.py:164
  440.2 3.3 bitcast_convert_fusion
  443.6 3.8 copy.83
  447.4 3.4 copy.91
  452.3 57.9 %reduce-scatter.10.cloned.1.call-done = bf16[128,512]{1,0:T(8,128)(2,1)} async-done(((bf16[2048,512]{1,0:T(8,128)(2,1)}), bf16[128,512]{1,0:T(8,128)(2,1)}) %reduce-scatter.10.cloned.1.call-update) | async-done | bytes 131088
  (93 shorter events, 18.6 us)
Async XLA Ops:
  7.2 64.5 %copy-start.5 = (bf16[1,2,128,256]{3,2,1,0:T(8,128)(2,1)S(1)}, bf16[1,2,128,256]{3,2,1,0:T(8,128)(2,1)}, u32[]{:S(2)}) copy-start(bf16[1,2,128,256]{3,2,1,0:T(8,128)(2,1)} %param.14) | copy-start | bytes 393220
  7.2 120.6 %reduce-scatter.6.cloned.1.call-start = ((), (), s32[]{:S(2)}) async-start(), calls=%async_computation.5 | async-start | bytes 557056 | tf_op jit(solution)/shard_map/reduce_scatter | solution.py:81
  37.7 35.7 %copy-start.4 = (bf16[128,128]{1,0:T(8,128)(2,1)}, bf16[128,128]{1,0:T(8,128)(2,1)S(1)}, u32[]{:S(2)}) copy-start(bf16[128,128]{1,0:T(8,128)(2,1)S(1)} %fusion.7) | copy-start | bytes 98308
  61.3 15.8 %copy-start.8 = (bf16[1,128,128]{2,1,0:T(8,128)(2,1)S(1)}, bf16[1,128,128]{2,1,0:T(8,128)(2,1)}, u32[]{:S(2)}) copy-start(bf16[1,128,128]{2,1,0:T(8,128)(2,1)} %param.13) | copy-start | bytes 98308
  61.3 8.4 %collective-permute-start = (bf16[128,1024]{1,0:T(8,128)(2,1)S(1)}, bf16[128,1024]{1,0:T(8,128)(2,1)S(1)}, u32[]{:S(2)}, u32[]{:S(2)}) collective-permute-start(bf16[128,1024]{1,0:T(8,128)(2,1)S(1)} %all_gather.25), channel_id=1, source_target_pairs={{0,128},{128,0},{256,384},{384,256},{1,129},{129,1},{257,385},{385... | collective-permute-start | bytes 786440 | tf_op jit(solution)/shard_map/ppermute | solution.py:17
  71.0 101.8 %all-gather.5.cloned.1.call-start = ((), (), s32[]{:S(2)}) async-start(), calls=%async_computation.6 | async-start | bytes 2228224 | tf_op jit(solution)/shard_map/all_gather | solution.py:108
  73.4 81.6 %all-to-all-start = ((bf16[128,16,128]{2,0,1:T(8,128)(2,1)}), bf16[128,16,128]{2,0,1:T(8,128)(2,1)S(1)}, u32[]{:S(2)}, u32[]{:S(2)}) async-start(bf16[128,16,128]{2,0,1:T(8,128)(2,1)} %maximum_select_fusion.1), calls=%async_computation.1 | async-start | bytes 1048576 | tf_op jit(solution)/shard_map/all_to_all | solution.py:97
  77.0 139.4 %all-gather.7.cloned.1.call-start = ((), (), s32[]{:S(2)}) async-start(), calls=%async_computation.7 | async-start | bytes 1179648 | tf_op jit(solution)/shard_map/all_gather | solution.py:111
  151.7 8.4 %collective-permute-start.1 = (bf16[128,1024]{1,0:T(8,128)(2,1)S(1)}, bf16[128,1024]{1,0:T(8,128)(2,1)}, u32[]{:S(2)}, u32[]{:S(2)}) collective-permute-start(bf16[128,1024]{1,0:T(8,128)(2,1)S(1)} %all_gather.26), channel_id=1, source_target_pairs={{0,128},{128,0},{256,384},{384,256},{1,129},{129,1},{257,385},{385... | collective-permute-start | bytes 786440 | tf_op jit(solution)/shard_map/ppermute | solution.py:17
  161.2 1.6 copy-start.1
  162.8 53.6 %copy-start.2 = (bf16[2,128,256]{2,1,0:T(8,128)(2,1)S(1)}, bf16[2,128,256]{2,1,0:T(8,128)(2,1)}, u32[]{:S(2)}) copy-start(bf16[2,128,256]{2,1,0:T(8,128)(2,1)} %bitcast_select_fusion) | copy-start | bytes 393220
  172.8 46.6 %copy-start.12 = (s32[15]{0:T(128)S(1)}, s32[15]{0:T(128)}, u32[]{:S(2)}) copy-start(s32[15]{0:T(128)} %param.9) | copy-start | bytes 184
  172.8 46.9 %copy-start.3 = (bf16[2,256,256]{2,1,0:T(8,128)(2,1)S(1)}, bf16[2,256,256]{2,1,0:T(8,128)(2,1)}, u32[]{:S(2)}) copy-start(bf16[2,256,256]{2,1,0:T(8,128)(2,1)} %param.16) | copy-start | bytes 786436
  176.4 44.0 %copy-start.9 = (s32[2,32]{1,0:T(2,128)S(1)}, s32[2,32]{1,0:T(2,128)}, u32[]{:S(2)}) copy-start(s32[2,32]{1,0:T(2,128)} %param.10) | copy-start | bytes 772
  176.4 44.2 %copy-start.11 = (s32[2]{0:T(128)S(1)}, s32[2]{0:T(128)}, u32[]{:S(2)}) copy-start(s32[2]{0:T(128)} %constant.94) | copy-start | bytes 28
  176.4 44.3 %copy-start.10 = (s32[2]{0:T(128)S(1)}, s32[2]{0:T(128)}, u32[]{:S(2)}) copy-start(s32[2]{0:T(128)} %constant.97) | copy-start | bytes 28
  176.4 110.0 %reduce-scatter.8.cloned.1.call-start = ((), (), s32[]{:S(2)}) async-start(), calls=%async_computation.8 | async-start | bytes 1114112 | tf_op jit(solution)/shard_map/reduce_scatter | solution.py:113
  216.4 4.4 copy-start
  219.2 11.2 %copy-start.7 = (bf16[1,256,128]{2,1,0:T(8,128)(2,1)S(1)}, bf16[1,256,128]{2,1,0:T(8,128)(2,1)}, u32[]{:S(2)}) copy-start(bf16[1,256,128]{2,1,0:T(8,128)(2,1)} %param.15) | copy-start | bytes 196612
  219.3 115.8 %all-gather.9.cloned.1.call-start = ((), (), s32[]{:S(2)}) async-start(), calls=%async_computation.9 | async-start | bytes 4456448 | tf_op jit(solution)/shard_map/all_gather | solution.py:150
  222.8 35.9 %all-to-all-start.1 = ((bf16[2,128,2048]{1,0,2:T(2,128)(2,1)}), bf16[2,128,2048]{1,0,2:T(2,128)(2,1)}, u32[]{:S(2)}, u32[]{:S(2)}) async-start(bf16[2,128,2048]{1,0,2:T(2,128)(2,1)} %copy.69), calls=%async_computation.3 | async-start | bytes 2097152 | tf_op jit(solution)/shard_map/all_to_all | solution.py:122
  230.4 209.9 %all-gather.11.cloned.1.call-start = ((), (), s32[]{:S(2)}) async-start(), calls=%async_computation.10 | async-start | bytes 3538944 | tf_op jit(solution)/shard_map/all_gather | solution.py:164
  382.7 127.6 %reduce-scatter.10.cloned.1.call-start = ((), (), s32[]{:S(2)}) async-start(), calls=%async_computation.11 | async-start | bytes 2228224
  447.4 64.0 %copy-start.6 = (bf16[2,256,128]{2,1,0:T(8,128)(2,1)S(1)}, bf16[2,256,128]{2,1,0:T(8,128)(2,1)}, u32[]{:S(2)}) copy-start(bf16[2,256,128]{2,1,0:T(8,128)(2,1)} %param.17) | copy-start | bytes 393220
Sparse Core Ops, SparseCore 0:
  71.1 56.6 reduce-scatter.5
  130.7 42.0 all-gather.4
  176.5 39.8 all-gather.6
  219.4 66.9 reduce-scatter.7
  288.9 46.0 all-gather.8
  382.8 57.3 all-gather.10
  450.9 59.3 reduce-scatter.9
where the time goes:
time: 520 us; the launch traced here: 519 us
  waiting for transfers between devices  293 us (56%)
  blocking collectives  97.1 us (19%)
  local copies, waits for them, and re-layouts  55.7 us (11%)
  other arithmetic  21.3 us (4%)
  matrix products  18.9 us (4%)
  starting transfers between devices  18.1 us (3%)
  between operations  14.6 us (3%)
    unnamed x8, waiting for transfers between devices  58.1 us
    all_gather x1, waiting for transfers between devices, local(): full_three = lax.all_gather(off_three, 'col', axis=3, tiled=True)  57.5 us
    unnamed x39, local copies, waits for them, and re-layouts  50.3 us
    reduce_scatter x1, waiting for transfers between devices, local(): lax.psum_scatter(term_one.astype(jnp.bfloat16), 'row', scatter_dimension=...  49.9 us
    all_gather x1, waiting for transfers between devices, local(): full_two = lax.all_gather(off_two, 'col', axis=2, tiled=True)  39.9 us
    all_gather x1, blocking collectives, local(): diag_rows_two = lax.all_gather(diag_two.T, 'col', axis=1, tiled=True)  25.9 us
    reduce_scatter x1, waiting for transfers between devices, local(): lax.psum_scatter(term_two.astype(jnp.bfloat16), 'row', scatter_dimension=...  25.3 us
    all_to_all x1, waiting for transfers between devices, local(): lax.all_to_all(full_two, 'row', split_axis=2, concat_axis=1, tiled=True)  24.9 us
  transfers between devices with their start and end apart: 11, of which 10 were waited for; matrix products, arithmetic and copies ran while one was open for 4% of the time, Pallas kernels for 0%

commit v1 on v0

--- a/solution.py
+++ b/solution.py
@@ -161,7 +161,9 @@
     )
     off_three = jnp.where(member[:, :, None], -product_three, 0.0).astype(jnp.bfloat16)
     off_three = off_three.reshape(bottom_dev, 3, rows_dev, own_cols)
-    full_three = lax.all_gather(off_three, "col", axis=3, tiled=True)
+    full_three = jnp.concatenate(
+        lax.all_to_all(jnp.stack([off_three] * lax.axis_size("col")), "col", 0, 0), axis=3
+    )
     term_three = jnp.einsum(
         "ekin,ekim->enm", chain_rows, full_three, preferred_element_type=jnp.float32
     )

time: 520 us -> 542 us (1.042)
  the two profiles are of different devices: /device:TPU:8 before, /device:TPU:2 now
where the time goes in v1:
time: 542 us; the launch traced here: 541 us
  waiting for transfers between devices  305 us (56%)
  blocking collectives  99.4 us (18%)
  local copies, waits for them, and re-layouts  58.1 us (11%)
  starting transfers between devices  23 us (4%)
  other arithmetic  22.6 us (4%)
  matrix products  17.9 us (3%)
  between operations  14.6 us (3%)
    all_to_all x1, waiting for transfers between devices, local(): lax.all_to_all(jnp.stack([off_three] * lax.axis_size('col')), 'col', 0, 0)  74.2 us
    unnamed x7, waiting for transfers between devices  54.6 us
    unnamed x45, local copies, waits for them, and re-layouts  51 us
    reduce_scatter x1, waiting for transfers between devices, local(): lax.psum_scatter(term_one.astype(jnp.bfloat16), 'row', scatter_dimension=...  48.9 us
    all_gather x1, waiting for transfers between devices, local(): full_two = lax.all_gather(off_two, 'col', axis=2, tiled=True)  39.9 us
    all_gather x1, blocking collectives, local(): diag_rows_two = lax.all_gather(diag_two.T, 'col', axis=1, tiled=True)  25.9 us
    reduce_scatter x1, waiting for transfers between devices, local(): lax.psum_scatter(term_two.astype(jnp.bfloat16), 'row', scatter_dimension=...  25.4 us
    all_to_all x1, waiting for transfers between devices, local(): lax.all_to_all(full_two, 'row', split_axis=2, concat_axis=1, tiled=True)  25 us
  transfers between devices with their start and end apart: 11, of which 10 were waited for; matrix products, arithmetic and copies ran while one was open for 4% of the time, Pallas kernels for 0%

profile of v1, /device:TPU:2, one launch (start us, length us, event | category | flops | bytes accessed | tf_op | source)
XLA Modules:
  0.0 540.5 jit_solution(8663510564523422827)
XLA Ops:
  10.2 24.6 %all_gather.21 = bf16[2048,128]{0,1:T(8,128)(2,1)S(1)} all-gather(bf16[128,128]{0,1:T(8,128)(2,1)S(1)} %bitcast_select_fusion.1), channel_id=1, replica_groups=mesh['leaf'=4,'row'=16,'col'=8] {'row'}, dimensions={0}, use_global_device_ids=true | all-gather | bytes 557056 | tf_op jit(solution)/shard_map/all_gather | solution.py:68
  38.3 25.0 %all_gather.22 = bf16[128,1024]{1,0:T(8,128)(2,1)S(1)} all-gather(bf16[128,128]{1,0:T(8,128)(2,1)S(1)} %fusion.7), channel_id=1, replica_groups=mesh['leaf'=4,'row'=16,'col'=8] {'col'}, dimensions={1}, use_global_device_ids=true | all-gather | bytes 294912 | tf_op jit(solution)/shard_map/all_gather | solution.py:71
  63.3 2.6 collective-permute-start
  65.9 5.8 %collective-permute-done = bf16[128,1024]{1,0:T(8,128)(2,1)S(1)} collective-permute-done((bf16[128,1024]{1,0:T(8,128)(2,1)S(1)}, bf16[128,1024]{1,0:T(8,128)(2,1)S(1)}, u32[]{:S(2)}, u32[]{:S(2)}) %collective-permute-start) | collective-permute-done | bytes 262176 | tf_op jit(solution)/shard_map/ppermute | solution.py:17
  75.4 3.6 all-to-all-start
  79.9 48.9 %reduce-scatter.6.cloned.1.call-done = bf16[128,128]{0,1:T(8,128)(2,1)} async-done(((bf16[128,2048]{0,1:T(8,128)(2,1)}), bf16[128,128]{0,1:T(8,128)(2,1)}) %reduce-scatter.6.cloned.1.call-update) | async-done | bytes 32784 | tf_op jit(solution)/shard_map/reduce_scatter | solution.py:81
  130.2 24.0 %all_gather.23 = bf16[128,1024]{1,0:T(8,128)(2,1)S(1)} all-gather(bf16[128,128]{1,0:T(8,128)(2,1)S(1)} %get-tuple-element.37), channel_id=1, replica_groups=mesh['leaf'=4,'row'=16,'col'=8] {'col'}, dimensions={1}, use_global_device_ids=true | all-gather | bytes 294912 | tf_op jit(solution)/shard_map/all_gather | solution.py:88
  154.2 2.3 collective-permute-start.1
  156.9 5.7 %collective-permute-done.1 = bf16[128,1024]{1,0:T(8,128)(2,1)} collective-permute-done((bf16[128,1024]{1,0:T(8,128)(2,1)S(1)}, bf16[128,1024]{1,0:T(8,128)(2,1)}, u32[]{:S(2)}, u32[]{:S(2)}) %collective-permute-start.1) | collective-permute-done | bytes 262176 | tf_op jit(solution)/shard_map/ppermute | solution.py:17
  165.3 8.1 %all-gather.4.cloned.1.call-done = bf16[2,2048,256]{2,1,0:T(8,128)(2,1)} async-done(((bf16[2,128,256]{2,1,0:T(8,128)(2,1)}), bf16[2,2048,256]{2,1,0:T(8,128)(2,1)}) %all-gather.4.cloned.1.call-update) | async-done | bytes 2097168 | tf_op jit(solution)/shard_map/all_gather | solution.py:108
  173.4 3.6 fusion.6
  177.1 39.9 %all-gather.6.cloned.1.call-done = bf16[2,128,2048]{2,1,0:T(8,128)(2,1)} async-done(((bf16[2,128,256]{2,1,0:T(8,128)(2,1)}), bf16[2,128,2048]{2,1,0:T(8,128)(2,1)}) %all-gather.6.cloned.1.call-update) | async-done | bytes 1048592 | tf_op jit(solution)/shard_map/all_gather | solution.py:111
  217.1 2.9 fusion.2
  221.5 2.0 copy.70
  223.5 7.5 %all-to-all-start.1 = ((bf16[2,128,2048]{1,0,2:T(2,128)(2,1)}), bf16[2,128,2048]{1,0,2:T(2,128)(2,1)}, u32[]{:S(2)}, u32[]{:S(2)}) async-start(bf16[2,128,2048]{1,0,2:T(2,128)(2,1)} %copy.70), calls=%async_computation.3 | async-start | bytes 2097152 | tf_op jit(solution)/shard_map/all_to_all | solution.py:122
  232.2 2.3 maximum_bitcast_fusion
  234.5 25.0 %all-to-all-done.1 = bf16[2,128,2048]{1,0,2:T(2,128)(2,1)} async-done(((bf16[2,128,2048]{1,0,2:T(2,128)(2,1)}), bf16[2,128,2048]{1,0,2:T(2,128)(2,1)}, u32[]{:S(2)}, u32[]{:S(2)}) %all-to-all-start.1) | async-done | bytes 1048608 | tf_op jit(solution)/shard_map/all_to_all | solution.py:122
  259.4 1.9 copy.98
  261.8 25.4 %reduce-scatter.8.cloned.1.call-done = bf16[256,128]{0,1:T(8,128)(2,1)} async-done(((bf16[256,2048]{0,1:T(8,128)(2,1)}), bf16[256,128]{0,1:T(8,128)(2,1)}) %reduce-scatter.8.cloned.1.call-update) | async-done | bytes 65552 | tf_op jit(solution)/shard_map/reduce_scatter | solution.py:113
  287.1 1.6 fusion.24
  288.7 25.9 %all_gather.27 = bf16[128,2048]{1,0:T(8,128)(2,1)S(1)} all-gather(bf16[128,256]{1,0:T(8,128)(2,1)S(1)} %get-tuple-element.35), channel_id=1, replica_groups=mesh['leaf'=4,'row'=16,'col'=8] {'col'}, dimensions={1}, use_global_device_ids=true | all-gather | bytes 589824 | tf_op jit(solution)/shard_map/all_gather | solution.py:121
  314.7 3.6 pad_maximum_fusion
  318.3 17.4 %all-gather.8.cloned.1.call-done = bf16[2,4096,256]{2,1,0:T(8,128)(2,1)} async-done(((bf16[2,256,256]{2,1,0:T(8,128)(2,1)}), bf16[2,4096,256]{2,1,0:T(8,128)(2,1)}) %all-gather.8.cloned.1.call-update) | async-done | bytes 4194320 | tf_op jit(solution)/shard_map/all_gather | solution.py:150
  335.8 39.1 %scatter_custom_fusion = bf16[12288,256]{1,0:T(8,128)(2,1)} fusion(s32[8192]{0:T(1024)S(1)} %bitcast.145, bf16[8192,256]{1,0:T(8,128)(2,1)} %bitcast.146, bf16[]{:T(256)} %constant.73.clone.1), kind=kCustom, calls=%fused_computation.3 | custom fusion | bytes 6291968
  374.8 7.6 %fusion.5 = bf16[2,384,256]{1,2,0:T(8,128)(2,1)S(1)} fusion(bf16[2,6144,256]{2,1,0:T(8,128)(2,1)} %bitcast.130, bf16[384,6144,1]{1,0,2:T(8,128)(2,1)} %bitcast.132, pred[2,384]{1,0:T(4,128)(4,1)S(1)} %compare_reduce_fusion), kind=kOutput, calls=%fused_computation.15 | convolution fusion | flops 2416508928 | bytes 11404032 | tf_op jit(solution)/shard_map/ab,ebn->ean/dot_general | solution.py:156
  382.6 2.1 stack.31
  384.7 6.7 %all-to-all-start.2 = ((bf16[8,2,3,128,256]{4,3,2,1,0:T(8,128)(2,1)}), bf16[8,2,3,128,256]{4,3,2,1,0:T(8,128)(2,1)S(1)}, u32[]{:S(2)}, u32[]{:S(2)}) async-start(bf16[8,2,3,128,256]{4,3,2,1,0:T(8,128)(2,1)} %stack.31), calls=%async_computation.4 | async-start | bytes 6291456 | tf_op jit(solution)/shard_map/all_to_all | solution.py:165
  391.5 74.2 %all-to-all-done.2 = bf16[8,2,3,128,256]{4,3,2,1,0:T(8,128)(2,1)S(1)} async-done(((bf16[8,2,3,128,256]{4,3,2,1,0:T(8,128)(2,1)}), bf16[8,2,3,128,256]{4,3,2,1,0:T(8,128)(2,1)S(1)}, u32[]{:S(2)}, u32[]{:S(2)}) %all-to-all-start.2) | async-done | bytes 3145760 | tf_op jit(solution)/shard_map/all_to_all | solution.py:165
  466.1 2.3 bitcast_convert_fusion
  468.4 3.8 copy.85
  472.3 3.4 copy.94
  477.3 54.6 %reduce-scatter.10.cloned.1.call-done = bf16[128,512]{1,0:T(8,128)(2,1)} async-done(((bf16[2048,512]{1,0:T(8,128)(2,1)}), bf16[128,512]{1,0:T(8,128)(2,1)}) %reduce-scatter.10.cloned.1.call-update) | async-done | bytes 131088
  (100 shorter events, 22.6 us)
Async XLA Ops:
  7.2 66.5 %copy-start.7 = (bf16[1,2,128,256]{3,2,1,0:T(8,128)(2,1)S(1)}, bf16[1,2,128,256]{3,2,1,0:T(8,128)(2,1)}, u32[]{:S(2)}) copy-start(bf16[1,2,128,256]{3,2,1,0:T(8,128)(2,1)} %param.14) | copy-start | bytes 393220
  7.2 121.6 %reduce-scatter.6.cloned.1.call-start = ((), (), s32[]{:S(2)}) async-start(), calls=%async_computation.6 | async-start | bytes 557056 | tf_op jit(solution)/shard_map/reduce_scatter | solution.py:81
  37.7 0.6 copy-start.6
  63.3 15.8 %copy-start.11 = (bf16[1,128,128]{2,1,0:T(8,128)(2,1)S(1)}, bf16[1,128,128]{2,1,0:T(8,128)(2,1)}, u32[]{:S(2)}) copy-start(bf16[1,128,128]{2,1,0:T(8,128)(2,1)} %param.13) | copy-start | bytes 98308
  63.3 8.4 %collective-permute-start = (bf16[128,1024]{1,0:T(8,128)(2,1)S(1)}, bf16[128,1024]{1,0:T(8,128)(2,1)S(1)}, u32[]{:S(2)}, u32[]{:S(2)}) collective-permute-start(bf16[128,1024]{1,0:T(8,128)(2,1)S(1)} %all_gather.22), channel_id=1, source_target_pairs={{0,128},{128,0},{256,384},{384,256},{1,129},{129,1},{257,385},{385... | collective-permute-start | bytes 786440 | tf_op jit(solution)/shard_map/ppermute | solution.py:17
  73.0 100.4 %all-gather.4.cloned.1.call-start = ((), (), s32[]{:S(2)}) async-start(), calls=%async_computation.7 | async-start | bytes 2228224 | tf_op jit(solution)/shard_map/all_gather | solution.py:108
  75.4 81.2 %all-to-all-start = ((bf16[128,16,128]{2,0,1:T(8,128)(2,1)}), bf16[128,16,128]{2,0,1:T(8,128)(2,1)S(1)}, u32[]{:S(2)}, u32[]{:S(2)}) async-start(bf16[128,16,128]{2,0,1:T(8,128)(2,1)} %maximum_select_fusion.1), calls=%async_computation.1 | async-start | bytes 1048576 | tf_op jit(solution)/shard_map/all_to_all | solution.py:97
  79.0 138.1 %all-gather.6.cloned.1.call-start = ((), (), s32[]{:S(2)}) async-start(), calls=%async_computation.8 | async-start | bytes 1179648 | tf_op jit(solution)/shard_map/all_gather | solution.py:111
  154.2 8.4 %collective-permute-start.1 = (bf16[128,1024]{1,0:T(8,128)(2,1)S(1)}, bf16[128,1024]{1,0:T(8,128)(2,1)}, u32[]{:S(2)}, u32[]{:S(2)}) collective-permute-start(bf16[128,1024]{1,0:T(8,128)(2,1)S(1)} %all_gather.23), channel_id=1, source_target_pairs={{0,128},{128,0},{256,384},{384,256},{1,129},{129,1},{257,385},{385... | collective-permute-start | bytes 786440 | tf_op jit(solution)/shard_map/ppermute | solution.py:17
  163.8 1.6 copy-start.1
  165.3 51.7 %copy-start.3 = (bf16[2,128,256]{2,1,0:T(8,128)(2,1)S(1)}, bf16[2,128,256]{2,1,0:T(8,128)(2,1)}, u32[]{:S(2)}) copy-start(bf16[2,128,256]{2,1,0:T(8,128)(2,1)} %bitcast_select_fusion) | copy-start | bytes 393220
  173.4 46.6 %copy-start.15 = (s32[15]{0:T(128)S(1)}, s32[15]{0:T(128)}, u32[]{:S(2)}) copy-start(s32[15]{0:T(128)} %param.9) | copy-start | bytes 184
  173.4 46.9 %copy-start.4 = (bf16[2,256,256]{2,1,0:T(8,128)(2,1)S(1)}, bf16[2,256,256]{2,1,0:T(8,128)(2,1)}, u32[]{:S(2)}) copy-start(bf16[2,256,256]{2,1,0:T(8,128)(2,1)} %param.16) | copy-start | bytes 786436
  177.1 44.0 %copy-start.12 = (s32[2,32]{1,0:T(2,128)S(1)}, s32[2,32]{1,0:T(2,128)}, u32[]{:S(2)}) copy-start(s32[2,32]{1,0:T(2,128)} %param.10) | copy-start | bytes 772
  177.1 44.2 %copy-start.14 = (s32[2]{0:T(128)S(1)}, s32[2]{0:T(128)}, u32[]{:S(2)}) copy-start(s32[2]{0:T(128)} %constant.94) | copy-start | bytes 28
  177.1 44.3 %copy-start.13 = (s32[2]{0:T(128)S(1)}, s32[2]{0:T(128)}, u32[]{:S(2)}) copy-start(s32[2]{0:T(128)} %constant.97) | copy-start | bytes 28
  177.1 110.0 %reduce-scatter.8.cloned.1.call-start = ((), (), s32[]{:S(2)}) async-start(), calls=%async_computation.9 | async-start | bytes 1114112 | tf_op jit(solution)/shard_map/reduce_scatter | solution.py:113
  217.1 4.4 copy-start
  219.9 11.2 %copy-start.10 = (bf16[1,256,128]{2,1,0:T(8,128)(2,1)S(1)}, bf16[1,256,128]{2,1,0:T(8,128)(2,1)}, u32[]{:S(2)}) copy-start(bf16[1,256,128]{2,1,0:T(8,128)(2,1)} %param.15) | copy-start | bytes 196612
  220.0 115.8 %all-gather.8.cloned.1.call-start = ((), (), s32[]{:S(2)}) async-start(), calls=%async_computation.10 | async-start | bytes 4456448 | tf_op jit(solution)/shard_map/all_gather | solution.py:150
  223.5 35.9 %all-to-all-start.1 = ((bf16[2,128,2048]{1,0,2:T(2,128)(2,1)}), bf16[2,128,2048]{1,0,2:T(2,128)(2,1)}, u32[]{:S(2)}, u32[]{:S(2)}) async-start(bf16[2,128,2048]{1,0,2:T(2,128)(2,1)} %copy.70), calls=%async_computation.3 | async-start | bytes 2097152 | tf_op jit(solution)/shard_map/all_to_all | solution.py:122
  382.6 2.1 copy-start.2
  384.7 81.0 %all-to-all-start.2 = ((bf16[8,2,3,128,256]{4,3,2,1,0:T(8,128)(2,1)}), bf16[8,2,3,128,256]{4,3,2,1,0:T(8,128)(2,1)S(1)}, u32[]{:S(2)}, u32[]{:S(2)}) async-start(bf16[8,2,3,128,256]{4,3,2,1,0:T(8,128)(2,1)} %stack.31), calls=%async_computation.4 | async-start | bytes 6291456 | tf_op jit(solution)/shard_map/all_to_all | solution.py:165
  391.5 140.3 %reduce-scatter.10.cloned.1.call-start = ((), (), s32[]{:S(2)}) async-start(), calls=%async_computation.11 | async-start | bytes 2228224
  472.3 3.5 copy-start.9
  472.3 4.2 copy-start.5
  472.3 60.6 %copy-start.8 = (bf16[2,256,128]{2,1,0:T(8,128)(2,1)S(1)}, bf16[2,256,128]{2,1,0:T(8,128)(2,1)}, u32[]{:S(2)}) copy-start(bf16[2,256,128]{2,1,0:T(8,128)(2,1)} %param.17) | copy-start | bytes 393220
Sparse Core Ops, SparseCore 0:
  73.1 55.5 reduce-scatter.5
  131.7 41.6 all-gather.3
  177.2 39.8 all-gather.5
  220.1 67.0 reduce-scatter.7
  289.7 46.0 all-gather.7
  475.8 55.9 reduce-scatter.9
